TPU v7x, 256 devices: a whole 4x4x8 slice. The times are simulated.
256 devices in a mesh: inner: 64 (over z_hi, y, x, core), outer: 4 (over z_lo).
Axes of the slice: x: 4, y: 4, z: 8 (z_hi: 2, z_lo: 4; z = z_hi * 4 + z_lo), core: 2. Of those that a mesh axis runs over, the one named last changes fastest.
Arguments:
- acts: bfloat16 [131072, 2048], P(('inner', 'outer')), may hold values from -24 to 24
- grad_out: bfloat16 [131072, 2048], P(('inner', 'outer')), may hold values from -6 to 6
- weight: bfloat16 [2048, 2048], P('inner'), may hold values from -0.125 to 0.125
- error: float32 [4, 2048, 2048], P('outer', 'inner'), may hold values from -4 to 4
- basis: float32 [2048, 64], replicated, may hold values from -6 to 6
Outputs:
- grad_acts: bfloat16 [131072, 2048], P(('inner', 'outer'))
- approx: float32 [2048, 2048], P('inner')
- error_new: float32 [4, 2048, 2048], P('outer', 'inner')
- factor_q: float32 [2048, 64], replicated
All inputs are finite; a program needn't handle non-finite values.
Results may differ from a plain program's by a relative error of at most 0.004.
Values may be sent and summed in bfloat16 or wider, within the bound.
A program may use at most 128 MiB of HBM per device.

v0:
```python
import math

import jax
import jax.numpy as jnp
from jax import lax
from jax.sharding import PartitionSpec as P


def orthonormal(factor_p, gram):
    lower = jnp.linalg.cholesky(gram)
    return jax.scipy.linalg.solve_triangular(lower, factor_p.T, lower=True).T


def shards(acts, grad_out, weight, error, basis):
    hi = lax.Precision.HIGHEST
    inner_count = lax.axis_size("inner")
    outer_count = lax.axis_size("outer")
    scale = 1.0 / math.sqrt(acts.shape[0] * inner_count)
    grad_acts = lax.dot_general(
        grad_out,
        lax.all_gather(weight, "inner", axis=0, tiled=True),
        (((1,), (1,)), ((), ())),
        preferred_element_type=jnp.float32,
    ).astype(jnp.bfloat16)
    grad_rows = lax.psum_scatter(
        lax.dot_general(
            acts, grad_out, (((0,), (0,)), ((), ())), preferred_element_type=jnp.float32
        )
        * scale,
        "inner",
        scatter_dimension=0,
        tiled=True,
    )
    merged = grad_rows + error[0]
    local_p = jnp.dot(merged, basis, precision=hi)
    factor_p = lax.psum(local_p, "outer") / outer_count
    gram = lax.psum(jnp.dot(factor_p.T, factor_p, precision=hi), "inner")
    ortho = orthonormal(factor_p, gram)
    local_q = lax.dot_general(
        merged, ortho, (((0,), (0,)), ((), ())), precision=hi, preferred_element_type=jnp.float32
    )
    factor_q = lax.psum(local_q, ("inner", "outer")) / outer_count
    approx = jnp.dot(ortho, factor_q.T, precision=hi)
    residue = merged - approx
    return (grad_acts, approx, residue[None], factor_q)


def solution(mesh):
    in_specs = (
        P(("inner", "outer"), None),
        P(("inner", "outer"), None),
        P("inner", None),
        P("outer", "inner", None),
        P(),
    )
    out_specs = (P(("inner", "outer"), None), P("inner", None), P("outer", "inner", None), P())
    return jax.shard_map(shards, mesh=mesh, in_specs=in_specs, out_specs=out_specs, check_vma=False)
```

profile of v0, /device:TPU:1, one launch (start us, length us, event | category | flops | bytes accessed | tf_op | source)
XLA Modules:
  0.0 1156.6 jit_solution(11408297317171306875)
XLA Ops:
  7.2 0.0 copy-start
  7.2 0.0 reduce-scatter.2.cloned.1.call-start
  7.2 1.5 copy-done
  8.8 9.7 convolution_multiply_fusion
  18.4 0.0 copy-start.1
  18.4 0.0 copy-start.5
  18.4 0.0 reduce-scatter.2.cloned.1.call-update
  18.5 0.0 all-gather.2.cloned.1.call-start
  18.5 0.7 all-gather.2.cloned.1.call-update
  19.2 0.0 all-reduce.2.cloned.1.call-start
  19.3 436.2 %reduce-scatter.2.cloned.1.call-done = f32[32,2048]{1,0:T(8,128)} async-done(((f32[2048,2048]{1,0:T(8,128)}), f32[32,2048]{1,0:T(8,128)}) %reduce-scatter.2.cloned.1.call-update) | async-done | bytes 262160 | tf_op jit(solution)/shard_map/reduce_scatter | solution.py:25
  455.4 0.0 copy-done.1
  455.4 0.0 copy-done.5
  455.4 1.5 fusion.12
  456.9 13.0 %psum.21 = f32[32,64]{1,0:T(8,128)S(1)} all-reduce(f32[32,64]{1,0:T(8,128)S(1)} %fusion.12), channel_id=1, replica_groups=mesh['inner'=64,'outer'=4] {'outer'}, use_global_device_ids=true, to_apply=%region_1.0 | all-reduce | flops 2048 | bytes 16384 | tf_op jit(solution)/shard_map/psum | solution.py:36
  470.0 0.2 fusion.5
  470.2 407.3 %psum.22 = f32[64,64]{0,1:T(8,128)S(1)} all-reduce(f32[64,64]{0,1:T(8,128)S(1)} %fusion.5), channel_id=1, replica_groups=mesh['inner'=64,'outer'=4] {'inner'}, use_global_device_ids=true, to_apply=%region_2.0 | all-reduce | flops 4096 | bytes 32768 | tf_op jit(solution)/shard_map/psum | solution.py:37
  877.5 0.1 copy.10
  877.6 5.8 cholesky.16
  883.5 0.6 compare_reduce_fusion
  884.1 0.7 fusion
  884.8 4.9 custom-call.7
  889.7 0.2 fusion.1
  889.8 2.4 fusion.11
  892.2 0.0 all-reduce.2.cloned.1.call-update
  892.2 0.0 copy-start.2
  892.2 0.0 all-gather.2.cloned.1.call-done
  892.3 9.1 convolution_convert_fusion
  901.4 246.4 %all-reduce.2.cloned.1.call-done = f32[2048,64]{0,1:T(8,128)} async-done(((f32[2048,64]{0,1:T(8,128)}), f32[2048,64]{0,1:T(8,128)}) %all-reduce.2.cloned.1.call-update) | async-done | bytes 524304 | tf_op jit(solution)/shard_map/psum | solution.py:42
  1147.8 1.1 broadcast_multiply_fusion
  1148.9 0.0 copy-start.3
  1148.9 0.4 fusion.13
  1149.3 0.0 copy-done.2
  1149.3 0.0 copy-start.4
  1149.3 0.8 subtract_bitcast_fusion
  1150.1 0.0 copy-done.3
  1150.1 0.0 copy-done.4
  (2 shorter events, 0.0 us)
Async XLA Ops:
  7.2 1.6 copy-start
  7.2 448.3 %reduce-scatter.2.cloned.1.call-start = ((), (), s32[]{:S(2)}) async-start(), calls=%async_computation.2 | async-start | bytes 17039360 | tf_op jit(solution)/shard_map/reduce_scatter | solution.py:25
  18.4 437.0 %copy-start.1 = (f32[1,32,2048]{2,1,0:T(8,128)S(1)}, f32[1,32,2048]{2,1,0:T(8,128)}, u32[]{:S(2)}) copy-start(f32[1,32,2048]{2,1,0:T(8,128)} %param.8) | copy-start | bytes 786436
  18.4 437.0 %copy-start.5 = (f32[2048,64]{0,1:T(8,128)S(1)}, f32[2048,64]{0,1:T(8,128)}, u32[]{:S(2)}) copy-start(f32[2048,64]{0,1:T(8,128)} %param.9) | copy-start | bytes 1572868
  18.5 873.8 %all-gather.2.cloned.1.call-start = ((), (), s32[]{:S(2)}) async-start(), calls=%async_computation.1 | async-start | bytes 8519680 | tf_op jit(solution)/shard_map/all_gather | solution.py:21
  19.2 1128.6 %all-reduce.2.cloned.1.call-start = ((), (), s32[]{:S(2)}) async-start(), calls=%async_computation.3 | async-start | bytes 1048576 | tf_op jit(solution)/shard_map/psum | solution.py:42
  892.2 257.1 %copy-start.2 = (f32[32,2048]{1,0:T(8,128)S(1)}, f32[32,2048]{1,0:T(8,128)}, u32[]{:S(2)}) copy-start(f32[32,2048]{1,0:T(8,128)} %reduce-scatter.2.cloned.1.call-done) | copy-start | bytes 786436
  1148.9 1.2 copy-start.3
  1149.3 0.8 copy-start.4
Sparse Core Ops, SparseCore 0:
  18.6 436.7 reduce-scatter.1
  459.1 114.8 all-gather.1
  892.3 255.4 all-reduce.1
where the time goes:
time: 1160 us
  waiting for transfers between devices  683 us (59%)
  blocking collectives  420 us (36%)
  matrix products  23.5 us (2%)
  other arithmetic  13.9 us (1%)
  between operations  13.9 us (1%)
    reduce_scatter x1, waiting for transfers between devices, shards(): lax.psum_scatter(lax.dot_general(acts, grad_out, (((0,), (0,)), ((), ()))...  436 us
    psum x1, blocking collectives, shards(): gram = lax.psum(jnp.dot(factor_p.T, factor_p, precision=hi), 'inner')  407 us
    psum x1, waiting for transfers between devices, shards(): factor_q = lax.psum(local_q, ('inner', 'outer')) / outer_count  246 us
  transfers between devices with their start and end apart: 3, of which 2 were waited for; matrix products, arithmetic and copies ran while one was open for 2% of the time, Pallas kernels for 0%

commit v1 on v0

v1 whole, which is shorter than its diff:
```python
import functools
import math

import jax
import jax.numpy as jnp
from jax import lax
from jax.experimental import pallas as pl
from jax.experimental.pallas import tpu as pltpu
from jax.sharding import PartitionSpec as P

F32 = jnp.float32
BF16 = jnp.bfloat16
HI = lax.Precision.HIGHEST
MESH = pl.DeviceIdType.MESH

TOK = 512
D = 2048
R = 64
GROUPS = 4
SEMS = 128


def nn(a, b, precision=None):
    return lax.dot_general(a, b, (((1,), (0,)), ((), ())), precision=precision, preferred_element_type=F32)


def nt(a, b, precision=None):
    return lax.dot_general(a, b, (((1,), (1,)), ((), ())), precision=precision, preferred_element_type=F32)


def split3(v):
    hi = v.astype(BF16)
    rest = v - hi.astype(F32)
    mid = rest.astype(BF16)
    lo = (rest - mid.astype(F32)).astype(BF16)
    return jnp.concatenate([hi, mid, lo], axis=0)


def fold3(v):
    return v[:R] + (v[R : 2 * R] + v[2 * R :])


def kernel(
    scale,
    acts_hbm, go_hbm, weight_hbm, error_hbm, basis_hbm,
    ga_hbm, approx_hbm, err_hbm, qt_hbm,
    acts, go, err, basis, W, AT, RT, go_tw, G, Gs, R1, R2, Q1, Q2, Z3, out, res,
    T, RC, A1, RX, A2, RY, RZ, F, M, osel, qt, apv,
    lsem, osem, ssem, rsem,
):
    i = lax.axis_index("inner")
    zl = lax.axis_index("outer")
    zh, y, x, c = i // 32, (i // 8) % 4, (i // 2) % 4, i % 2
    z = zh * 4 + zl

    def dev(zh_, y_, x_, c_, zl_):
        return (((zh_ * 4 + y_) * 4 + x_) * 2 + c_, zl_)

    def at_x(d):
        return dev(zh, y, (x + d) % 4, c, zl)

    def at_y(d):
        return dev(zh, (y + d) % 4, x, c, zl)

    def at_z(d):
        zz = (z + d) % 8
        return dev(zz // 4, y, x, c, zz % 4)

    twin = dev(zh, y, x, 1 - c, zl)
    mirror = dev(1 - zh, y, x, c, 3 - zl)

    count = [0]
    sent = []

    def send(src, dst, to):
        k = count[0]
        count[0] += 1
        cp = pltpu.make_async_remote_copy(
            src_ref=src, dst_ref=dst, send_sem=ssem.at[k], recv_sem=rsem.at[k], device_id=to, device_id_type=MESH
        )
        cp.start()
        sent.append(cp)
        return cp

    wl = [pltpu.make_async_copy(weight_hbm.at[pl.ds(16 * h, 16)], W.at[zh, y, x, c, h], lsem.at[h]) for h in range(2)]
    gl = pltpu.make_async_copy(go_hbm, go, lsem.at[2])
    al = pltpu.make_async_copy(acts_hbm, acts, lsem.at[3])
    bl = pltpu.make_async_copy(basis_hbm, basis, lsem.at[4])
    el = pltpu.make_async_copy(error_hbm, err, lsem.at[5])
    for cp in wl + [bl, gl, al, el]:
        cp.start()

    barrier = pltpu.get_barrier_semaphore()
    peers = [twin] + [at_x(d) for d in (1, 2, 3)] + [at_y(d) for d in (1, 2, 3)] + [at_z(d) for d in range(1, 8)]
    for p in peers:
        pl.semaphore_signal(barrier, inc=1, device_id=p, device_id_type=MESH)
    pl.semaphore_wait(barrier, len(peers))

    def gather(own, h):
        zs = zh if own else 1 - zh
        if h == 0:
            me1, me2, ax1, ax2 = x, y, at_x, at_y
        else:
            me1, me2, ax1, ax2 = y, x, at_y, at_x

        def piece(a):
            return W.at[zs, y, a % 4, c, 0] if h == 0 else W.at[zs, a % 4, x, c, 1]

        def block(b):
            return W.at[zs, b % 4, :, c, 0] if h == 0 else W.at[zs, :, b % 4, c, 1]

        p = piece(me1)
        up = send(p, p, ax1(1))
        down = send(p, p, ax1(3))
        yield
        up.wait_recv()
        if own:
            p = piece(me1 + 3)
            far = send(p, p, ax1(1))
        down.wait_recv()
        if not own:
            p = piece(me1 + 1)
            far = send(p, p, ax1(3))
        yield
        far.wait_recv()
        b = block(me2)
        up = send(b, b, ax2(1))
        down = send(b, b, ax2(3))
        tw = [send(b, b, twin)]
        yield
        up.wait_recv()
        b = block(me2 + 3)
        if own:
            far = send(b, b, ax2(1))
        tw.append(send(b, b, twin))
        down.wait_recv()
        b = block(me2 + 1)
        if not own:
            far = send(b, b, ax2(3))
        tw.append(send(b, b, twin))
        yield
        far.wait_recv()
        b = block(me2 + 2)
        tw.append(send(b, b, twin))
        yield
        for cp in tw:
            cp.wait_recv()
        yield

    def add_to(dst_f32, dst_bf16, terms, n):
        def body(j, carry):
            v = dst_f32[j]
            for t in terms:
                v = v + t[j].astype(F32)
            if dst_bf16 is not None:
                dst_bf16[j] = v.astype(BF16)
            return carry

        lax.fori_loop(0, n, body, 0)

    def scatter(h):
        if h == 0:
            me1, me2, ax1, ax2 = x, y, at_x, at_y
        else:
            me1, me2, ax1, ax2 = y, x, at_y, at_x

        def one(buf, a, s):
            return buf.at[a % 4, s, :, 0] if h == 0 else buf.at[:, s, a % 4, 1]

        def two(buf, b, s):
            return buf.at[x, s, b % 4, 0] if h == 0 else buf.at[b % 4, s, y, 1]

        far_p = send(one(Gs, me1 + 2, 0), R2.at[h, 0], ax1(1))
        far_m = send(one(Gs, me1 + 2, 1), R2.at[h, 1], ax1(3))
        near_p = send(one(Gs, me1 + 1, 1), R1.at[h, 0, 1], ax1(1))
        near_m = send(one(Gs, me1 + 3, 0), R1.at[h, 1, 0], ax1(3))
        yield
        far_p.wait_recv()
        add_to(one(G, me1 + 1, 0), one(Gs, me1 + 1, 0), [R2.at[h, 0]], 4)
        both_p = send(one(Gs, me1 + 1, 0), R1.at[h, 0, 0], ax1(1))
        far_m.wait_recv()
        add_to(one(G, me1 + 3, 1), one(Gs, me1 + 3, 1), [R2.at[h, 1]], 4)
        both_m = send(one(Gs, me1 + 3, 1), R1.at[h, 1, 1], ax1(3))
        yield
        near_p.wait_recv()
        near_m.wait_recv()
        both_p.wait_recv()
        both_m.wait_recv()
        for s in range(2):
            g, gs, ra, rb = one(G, me1, s), one(Gs, me1, s), R1.at[h, 0, s], R1.at[h, 1, s]

            def body(j, carry):
                v = g[j] + ra[j].astype(F32) + rb[j].astype(F32)
                g[j] = v
                gs[j] = v.astype(BF16)
                return carry

            lax.fori_loop(0, 4, body, 0)
        far_p = send(two(Gs, me2 + 2, 0), Q2.at[h, 0], ax2(1))
        far_m = send(two(Gs, me2 + 2, 1), Q2.at[h, 1], ax2(3))
        near_p = send(two(Gs, me2 + 1, 1), Q1.at[h, 0, 1], ax2(1))
        near_m = send(two(Gs, me2 + 3, 0), Q1.at[h, 1, 0], ax2(3))
        yield
        far_p.wait_recv()
        two(Gs, me2 + 1, 0)[...] = (two(G, me2 + 1, 0)[...] + Q2[h, 0].astype(F32)).astype(BF16)
        both_p = send(two(Gs, me2 + 1, 0), Q1.at[h, 0, 0], ax2(1))
        far_m.wait_recv()
        two(Gs, me2 + 3, 1)[...] = (two(G, me2 + 3, 1)[...] + Q2[h, 1].astype(F32)).astype(BF16)
        both_m = send(two(Gs, me2 + 3, 1), Q1.at[h, 1, 1], ax2(3))
        yield
        near_p.wait_recv()
        near_m.wait_recv()
        both_p.wait_recv()
        both_m.wait_recv()
        away = 1 - zh
        two(Gs, me2, away)[...] = (
            two(G, me2, away)[...] + Q1[h, 0, away].astype(F32) + Q1[h, 1, away].astype(F32)
        ).astype(BF16)
        last = send(two(Gs, me2, away), Z3.at[h], at_z(4))
        yield
        mine = two(G, me2, zh)[...] + Q1[h, 0, zh].astype(F32) + Q1[h, 1, zh].astype(F32)
        last.wait_recv()
        res[pl.ds(16 * h, 16), :] = mine + Z3[h].astype(F32)
        yield

    def allreduce(k):
        cp = send(T.at[k, pl.ds((1 - c) * 4, 4)], RC.at[k], twin)
        yield
        cp.wait_recv()
        A1[k] = T[k, pl.ds(c * 4, 4)] + RC[k]
        cps = [send(A1.at[k, (x + d) % 4], RX.at[k, d - 1], at_x(d)) for d in (2, 1, 3)]
        yield
        for cp in cps:
            cp.wait_recv()
        v = (A1[k, x] + RX[k, 0]) + (RX[k, 1] + RX[k, 2])
        for j in range(4):
            A2[k, j] = v[:, 512 * j : 512 * (j + 1)]
        cps = [send(A2.at[k, (y + d) % 4], RY.at[k, d - 1], at_y(d)) for d in (2, 1, 3)]
        yield
        for cp in cps:
            cp.wait_recv()
        RZ[k, z] = (A2[k, y] + RY[k, 0]) + (RY[k, 1] + RY[k, 2])
        cps = [send(RZ.at[k, z], RZ.at[k, z], at_z(d)) for d in (4, 3, 5, 2, 6, 1, 7)]
        yield
        for cp in cps:
            cp.wait_recv()
        v = ((RZ[k, 0] + RZ[k, 1]) + (RZ[k, 2] + RZ[k, 3])) + ((RZ[k, 4] + RZ[k, 5]) + (RZ[k, 6] + RZ[k, 7]))
        cx = c * 4 + x
        F[k, cx, y] = v
        cps = [send(F.at[k, cx, y], F.at[k, cx, y], at_y(d)) for d in (2, 1, 3)]
        yield
        for cp in cps:
            cp.wait_recv()
        cps = [send(F.at[k, cx], F.at[k, cx], at_x(d)) for d in (2, 1, 3)]
        yield
        for cp in cps:
            cp.wait_recv()
        half = F.at[k, pl.ds(c * 4, 4)]
        cp = send(half, half, twin)
        yield
        cp.wait_recv()
        yield

    def full(k):
        return jnp.concatenate([F[k, :, j].reshape(R, 512) for j in range(4)], axis=1)

    def put(k, v):
        T[k] = v.reshape(8, 8, D)

    def my_block(k):
        v = F[k, :, i // 16].reshape(R, 512)
        quarter = (i // 4) % 4
        blk = v[:, :128]
        for j in range(1, 4):
            blk = jnp.where(quarter == j, v[:, 128 * j : 128 * (j + 1)], blk)
        return blk

    def err_rows():
        e = err[...]
        row = lax.broadcasted_iota(jnp.int32, (128, D), 0)
        return jnp.where(row // 32 == i % 4, jnp.concatenate([e] * 4, axis=0), 0.0)

    weight_own = [gather(True, h) for h in range(2)]
    weight_oth = [gather(False, h) for h in range(2)]
    grads = [scatter(h) for h in range(2)]
    red = [allreduce(k) for k in range(2)]

    def adv(*gens):
        for g in gens:
            next(g)

    def transpose_acts():
        for b in range(8):
            t = acts[:, 256 * b : 256 * (b + 1)].T
            for j in range(8):
                AT[j % 2, j // 2, pl.ds(32 * b, 32)] = t[32 * j : 32 * (j + 1)]

    def left_factor():
        basis_t = basis[...].T
        b3 = split3(basis_t)
        u = fold3(nt(b3, go[...]))
        p = fold3(nn(split3(u), acts[...]))
        el.wait()
        eb = nt(basis_t, err_rows(), HI)
        col = lax.broadcasted_iota(jnp.int32, (R, D), 1)
        eb = jnp.where(col // 128 == i // 4, jnp.concatenate([eb] * 16, axis=1), 0.0)
        put(0, (p * scale + eb) * (1.0 / GROUPS))

    def right_factor():
        pt = full(0)
        v = fold3(nt(split3(pt), acts[...]))
        s = fold3(nn(split3(v), go[...]))
        pe = nn(my_block(0), err_rows(), HI)
        put(1, (s * scale + pe) * (1.0 / GROUPS))

    def gram():
        pt = full(0)
        row = lax.broadcasted_iota(jnp.int32, (R, R), 0)
        col = lax.broadcasted_iota(jnp.int32, (R, R), 1)
        M[...] = jnp.concatenate([nt(pt, pt, HI), (row == col).astype(F32)], axis=1)

    def factor(lo, hi):
        row = lax.broadcasted_iota(jnp.int32, (R, 2 * R), 0)
        col = lax.broadcasted_iota(jnp.int32, (R, 2 * R), 1)

        def body(k, m):
            rk = jnp.sum(jnp.where(row == k, m, 0.0), axis=0, keepdims=True)
            ck = jnp.sum(jnp.where(col == k, m, 0.0), axis=1, keepdims=True)
            piv = jnp.sum(jnp.where(col[:1] == k, rk, 0.0), axis=1, keepdims=True)
            rk = rk / jnp.sqrt(piv)
            ck = ck / jnp.sqrt(piv)
            return jnp.where(row > k, m - ck * rk, jnp.where(row == k, rk, m))

        M[...] = lax.fori_loop(lo, hi, body, M[...])

    def grad_own(d):
        a = (x + d) % 4

        def body(n, carry):
            cols = pl.ds(pl.multiple_of(n * 512, 512), 512)
            v = nn(AT[c, a], go[:, cols])
            G[a, :, :, :, :, cols] = v.reshape(2, 4, 2, 16, 512)
            return carry

        lax.fori_loop(0, 4, body, 0)

    def grad_twin(d):
        a = (x + d) % 4

        def body(n, carry):
            cols = pl.ds(pl.multiple_of(n * 512, 512), 512)
            v = nn(RT[a], go_tw[:, cols]).reshape(2, 4, 2, 16, 512)
            v = (v + G[a, :, :, :, :, cols]) * scale
            G[a, :, :, :, :, cols] = v
            Gs[a, :, :, :, :, cols] = v.astype(BF16)
            return carry

        lax.fori_loop(0, 4, body, 0)

    outs = []

    def grad_acts(s, d):
        b = (y + d) % 4
        w = W[s, b].reshape(256, D)
        j = s * 4 + b
        out[j] = nt(go[...], w).astype(BF16)
        cp = pltpu.make_async_copy(out.at[j], ga_hbm.at[:, pl.ds(pl.multiple_of(j * 256, 256), 256)], osem.at[len(outs)])
        cp.start()
        outs.append(cp)

    for cp in wl:
        cp.wait()
    wz = send(W.at[zh, y, x, c], W.at[zh, y, x, c], mirror)
    adv(*weight_own)
    gl.wait()
    got = send(go, go_tw, twin)
    bl.wait()
    al.wait()
    left_factor()
    adv(red[0])
    transpose_acts()
    att = send(AT.at[1 - c], RT, twin)
    wz.wait_recv()
    adv(*weight_oth)
    adv(*weight_own)
    adv(red[0])
    adv(*weight_oth)
    grad_own(2)
    grad_own(1)
    adv(*weight_own)
    adv(red[0])
    grad_own(3)
    grad_own(0)
    adv(red[0])
    got.wait_recv()
    att.wait_recv()
    grad_twin(2)
    grad_twin(1)
    adv(red[0])
    grad_twin(3)
    grad_twin(0)
    adv(*grads)
    adv(red[0])
    adv(*weight_oth)
    adv(red[0])
    adv(red[0])
    right_factor()
    adv(red[1])
    adv(*grads)
    gram()
    adv(red[1])
    factor(0, 16)
    adv(red[1])
    adv(*weight_own)
    factor(16, 32)
    adv(red[1])
    adv(*grads)
    factor(32, 48)
    adv(red[1])
    factor(48, 64)
    adv(*weight_oth)
    adv(red[1])
    adv(*grads)
    adv(red[1])
    adv(*grads)
    adv(*weight_own)
    adv(red[1])
    adv(*weight_oth)
    inv = M[:, R:]
    qf = nn(inv, full(1), HI)
    qt[...] = qf
    qcp = pltpu.make_async_copy(qt, qt_hbm, lsem.at[6])
    qcp.start()
    ot = nn(inv, my_block(0), HI)
    osel[...] = ot.T.reshape(4, 32, R)
    ap = nn(osel[i % 4], qf, HI)
    apv[...] = ap
    acp = pltpu.make_async_copy(apv, approx_hbm, lsem.at[7])
    acp.start()
    adv(*weight_own)
    adv(*weight_oth)
    for s in range(2):
        for d in range(4):
            grad_acts(s, d)
    adv(*grads)
    e = res[...] + err[...] - ap
    res[...] = e
    ecp = pltpu.make_async_copy(res, err_hbm, lsem.at[8])
    ecp.start()

    for cp in outs + [qcp, acp, ecp]:
        cp.wait()
    for cp in sent:
        cp.wait_send()
    assert count[0] <= SEMS, count[0]


def shards(acts, grad_out, weight, error, basis):
    scale = 1.0 / math.sqrt(TOK * lax.axis_size("inner"))
    anyspace = pl.BlockSpec(memory_space=pl.ANY)
    vm = pltpu.VMEM
    ga, approx, err, qt = pl.pallas_call(
        functools.partial(kernel, scale),
        out_shape=(
            jax.ShapeDtypeStruct((TOK, D), BF16),
            jax.ShapeDtypeStruct((32, D), F32),
            jax.ShapeDtypeStruct((32, D), F32),
            jax.ShapeDtypeStruct((R, D), F32),
        ),
        in_specs=[anyspace] * 5,
        out_specs=(anyspace,) * 4,
        scratch_shapes=[
            vm((TOK, D), BF16),
            vm((TOK, D), BF16),
            vm((32, D), F32),
            vm((D, R), F32),
            vm((2, 4, 4, 2, 2, 16, D), BF16),
            vm((2, 4, 256, TOK), BF16),
            vm((4, 256, TOK), BF16),
            vm((TOK, D), BF16),
            vm((4, 2, 4, 2, 16, D), F32),
            vm((4, 2, 4, 2, 16, D), BF16),
            vm((2, 2, 2, 4, 16, D), BF16),
            vm((2, 2, 4, 16, D), BF16),
            vm((2, 2, 2, 16, D), BF16),
            vm((2, 2, 16, D), BF16),
            vm((2, 16, D), BF16),
            vm((8, TOK, 256), BF16),
            vm((32, D), F32),
            vm((2, 8, 8, D), F32),
            vm((2, 4, 8, D), F32),
            vm((2, 4, 8, D), F32),
            vm((2, 3, 8, D), F32),
            vm((2, 4, 8, 512), F32),
            vm((2, 3, 8, 512), F32),
            vm((2, 8, 8, 512), F32),
            vm((2, 8, 4, 8, 512), F32),
            vm((R, 2 * R), F32),
            vm((4, 32, R), F32),
            vm((R, D), F32),
            vm((32, D), F32),
            pltpu.SemaphoreType.DMA((9,)),
            pltpu.SemaphoreType.DMA((8,)),
            pltpu.SemaphoreType.DMA((SEMS,)),
            pltpu.SemaphoreType.DMA((SEMS,)),
        ],
        compiler_params=pltpu.CompilerParams(
            collective_id=0, has_side_effects=True, vmem_limit_bytes=60 * 2**20
        ),
        name="powersgd",
    )(acts, grad_out, weight, error[0], basis)
    return (ga, approx, err[None], qt.T)


def solution(mesh):
    in_specs = (
        P(("inner", "outer"), None),
        P(("inner", "outer"), None),
        P("inner", None),
        P("outer", "inner", None),
        P(),
    )
    out_specs = (P(("inner", "outer"), None), P("inner", None), P("outer", "inner", None), P())
    return jax.shard_map(shards, mesh=mesh, in_specs=in_specs, out_specs=out_specs, check_vma=False)
```

time: 1160 us -> 109 us (0.09)
  waiting for transfers between devices: 683 us -> 0 us
  blocking collectives: 420 us -> 0 us
  Pallas kernels: 0 us -> 101 us
  matrix products: 23.5 us -> 0 us
  other arithmetic: 13.9 us -> 0 us
  between operations: 13.9 us -> 0.67 us
    reduce_scatter x1 -> x0, waiting for transfers between devices: 436 us -> none  [shards(): lax.psum_scatter(lax.dot_general(acts, grad_out, (((0,), (0,)), ((), ()))...]
    psum x2 -> x0, blocking collectives: 420 us -> none  [the longest x1 407 us: shards(): gram = lax.psum(jnp.dot(factor_p.T, factor_p, precision=hi), 'inner')]
    psum x1 -> x0, waiting for transfers between devices: 246 us -> none  [shards(): factor_q = lax.psum(local_q, ('inner', 'outer')) / outer_count]
    pallas_call x0 -> x1, Pallas kernels: none -> 101 us  [shards(): pl.pallas_call(functools.partial(kernel, scale), out_shape=(jax.ShapeDtyp...]
    dot_general x6 -> x0, matrix products: 23.3 us -> none  [the longest x1 9.67 us: shards(): lax.dot_general(acts, grad_out, (((0,), (0,)), ((), ())), preferred_eleme...]
    another operation x5 -> x0, other arithmetic: 12.1 us -> none  [the longest x3 6.52 us: orthonormal(): lower = jnp.linalg.cholesky(gram)]
  transfers between devices with their start and end apart: 3 -> 0, of which waited for: 2 -> 0; matrix products, arithmetic and copies ran while one was open for 2% -> 0% of each run, Pallas kernels for 0% -> 0%
where the time goes in v1:
time: 109 us
  Pallas kernels  101 us (93%)
  local copies, waits for them, and re-layouts  7.81 us (7%)
    pallas_call x1, Pallas kernels, shards(): pl.pallas_call(functools.partial(kernel, scale), out_shape=(jax.ShapeDtyp...  101 us
    unnamed x11, local copies, waits for them, and re-layouts  7.81 us

profile of v1, /device:TPU:1, one launch (start us, length us, event | category | flops | bytes accessed | tf_op | source)
XLA Modules:
  0.0 109.0 jit_solution(4558672834053432863)
XLA Ops:
  0.6 2.4 %copy.9.basis_hbm = f32[2048,64]{1,0:T(8,128)} copy(f32[2048,64]{0,1:T(8,128)} %param.9) | data formatting | bytes 1048576 | tf_op args[4]
  3.0 100.5 %powersgd.1 = (bf16[512,2048]{1,0:T(8,128)(2,1)}, f32[32,2048]{1,0:T(8,128)}, f32[32,2048]{1,0:T(8,128)}, f32[64,2048]{1,0:T(8,128)}) custom-call(bf16[512,2048]{1,0:T(8,128)(2,1)} %acts_hbm.1, bf16[512,2048]{1,0:T(8,128)(2,1)} %go_hbm.1, bf16[32,2048]{1,0:T(8,128)(2,1)} %weight_hbm.1, f32[32,2048]{1,0:T(8,128)} %bitcast.4, f32[2048,64]{1,0:T(8,128)} %copy.9.basis_hbm), custom_call_target="tpu_custom_call" | custom-call | tf_op jit(solution)/shard_map/powersgd/pallas_call | solution.py:462
  103.5 0.0 copy-start.2
  103.5 0.0 copy-start.1
  103.6 0.0 copy-start
  103.6 3.2 %copy.14 = bf16[512,2048]{1,0:T(8,128)(2,1)} copy(bf16[512,2048]{1,0:T(8,128)(2,1)} %get-tuple-element.16) | data formatting | bytes 4194304
  106.8 0.0 copy-done.2
  106.8 0.7 copy.15
  107.5 0.0 copy-done.1
  107.5 0.7 copy.16
  108.2 0.0 copy-done
  108.2 0.8 copy.17
Async XLA Ops:
  103.5 3.3 %copy-start.2 = (f32[32,2048]{1,0:T(8,128)S(1)}, f32[32,2048]{1,0:T(8,128)}, u32[]{:S(2)}) copy-start(f32[32,2048]{1,0:T(8,128)} %get-tuple-element.17) | copy-start | bytes 786436
  103.5 4.0 %copy-start.1 = (f32[32,2048]{1,0:T(8,128)S(1)}, f32[32,2048]{1,0:T(8,128)}, u32[]{:S(2)}) copy-start(f32[32,2048]{1,0:T(8,128)} %get-tuple-element.10) | copy-start | bytes 786436
  103.6 4.7 %copy-start = (f32[64,2048]{1,0:T(8,128)S(1)}, f32[64,2048]{1,0:T(8,128)}, u32[]{:S(2)}) copy-start(f32[64,2048]{1,0:T(8,128)} %get-tuple-element.11) | copy-start | bytes 1572868

commit v2 on v1

v2 whole, which is shorter than its diff:
```python
import functools
import math

import jax
import jax.numpy as jnp
from jax import lax
from jax.experimental import pallas as pl
from jax.experimental.pallas import tpu as pltpu
from jax.sharding import PartitionSpec as P

F32 = jnp.float32
BF16 = jnp.bfloat16
HI = lax.Precision.HIGHEST
MESH = pl.DeviceIdType.MESH

TOK = 512
D = 2048
R = 64
GROUPS = 4
SEMS = 96


def nn(a, b, precision=None):
    return lax.dot_general(a, b, (((1,), (0,)), ((), ())), precision=precision, preferred_element_type=F32)


def nt(a, b, precision=None):
    return lax.dot_general(a, b, (((1,), (1,)), ((), ())), precision=precision, preferred_element_type=F32)


def split3(v):
    hi = v.astype(BF16)
    rest = v - hi.astype(F32)
    mid = rest.astype(BF16)
    lo = (rest - mid.astype(F32)).astype(BF16)
    return jnp.concatenate([hi, mid, lo], axis=0)


def fold3(v):
    return v[:R] + (v[R : 2 * R] + v[2 * R :])


def kernel(
    scale,
    acts_hbm, go_hbm, weight_hbm, error_hbm, basis_hbm,
    ga, apv, res, qt,
    acts, go, err, basis, WA, WC, AT, RT, go_tw, G, Gs, R1, R2, Q1, Q2, Z3,
    T, RC, A1, RP, RZ, F, M,
    lsem, ssem, rsem,
):
    i = lax.axis_index("inner")
    zl = lax.axis_index("outer")
    zh, y, x, c = i // 32, (i // 8) % 4, (i // 2) % 4, i % 2
    z = zh * 4 + zl

    def dev(zh_, y_, x_, c_, zl_):
        return (((zh_ * 4 + y_) * 4 + x_) * 2 + c_, zl_)

    def at_x(d):
        return dev(zh, y, (x + d) % 4, c, zl)

    def at_y(d):
        return dev(zh, (y + d) % 4, x, c, zl)

    def at_xy(dx, dy):
        return dev(zh, (y + dy) % 4, (x + dx) % 4, c, zl)

    def at_z(d):
        zz = (z + d) % 8
        return dev(zz // 4, y, x, c, zz % 4)

    twin = dev(zh, y, x, 1 - c, zl)
    mirror = dev(1 - zh, y, x, c, 3 - zl)
    plane = sorted(
        [(dx, dy) for dx in range(4) for dy in range(4) if dx or dy],
        key=lambda p: -(min(p[0], 4 - p[0]) + min(p[1], 4 - p[1])),
    )

    count = [0]
    sent = []

    def copy(src, dst, to, k=None):
        if k is None:
            k = count[0]
            count[0] += 1
        return pltpu.make_async_remote_copy(
            src_ref=src, dst_ref=dst, send_sem=ssem.at[k], recv_sem=rsem.at[k], device_id=to, device_id_type=MESH
        )

    def send(src, dst, to):
        cp = copy(src, dst, to)
        cp.start()
        sent.append(cp)
        return cp

    def group(size):
        k = count[0]
        count[0] += 1
        return k, copy(size, size, twin, k)

    def send_group(size, copies):
        k, whole = group(size)
        for src, dst, to in copies:
            copy(src, dst, to, k).start()
        sent.append(whole)
        return whole

    source = (x + y) % 4 == zl
    wl = [
        pltpu.make_async_copy(weight_hbm.at[pl.ds(0, 16)], WA.at[zh, y, x, c], lsem.at[0]),
        pltpu.make_async_copy(weight_hbm.at[pl.ds(16, 16)], WC.at[z, c, y], lsem.at[1]),
    ]
    gl = pltpu.make_async_copy(go_hbm, go, lsem.at[2])
    al = pltpu.make_async_copy(acts_hbm, acts, lsem.at[3])
    bl = pltpu.make_async_copy(basis_hbm, basis, lsem.at[4])
    el = pltpu.make_async_copy(error_hbm, err, lsem.at[5])
    wl[0].start()
    pl.when(source)(wl[1].start)
    for cp in (bl, gl, al, el):
        cp.start()

    barrier = pltpu.get_barrier_semaphore()
    peers = [twin] + [at_xy(*p) for p in plane] + [at_z(d) for d in range(1, 8)]
    for p in peers:
        pl.semaphore_signal(barrier, inc=1, device_id=p, device_id_type=MESH)

    def gather(own, half):
        zs = zh if own else 1 - zh
        cols = pl.ds(half * (D // 2), D // 2)
        if half == 0:
            me1, me2, ax1, ax2 = x, y, at_x, at_y
        else:
            me1, me2, ax1, ax2 = y, x, at_y, at_x

        def piece(a):
            return WA.at[zs, y, a % 4, c, :, cols] if half == 0 else WA.at[zs, a % 4, x, c, :, cols]

        def block(b, lo=0, n=4):
            if half == 0:
                return WA.at[zs, b % 4, pl.ds(lo, n), c, :, cols]
            return WA.at[zs, pl.ds(lo, n), b % 4, c, :, cols]

        p = piece(me1)
        up = send(p, p, ax1(1))
        down = send(p, p, ax1(3))
        yield
        up.wait_recv()
        p = piece(me1 + 3)
        far = send(p, p, ax1(1))
        down.wait_recv()
        yield
        far.wait_recv()
        b = block(me2)
        up = send(b, b, ax2(1))
        down = send(b, b, ax2(3))
        k, tw = group(WA.at[0, :, :, 0, :, cols])
        copy(b, b, twin, k).start()
        yield
        up.wait_recv()
        b = block(me2 + 3, 0, 2)
        far_p = send(b, b, ax2(1))
        b = block(me2 + 3)
        copy(b, b, twin, k).start()
        down.wait_recv()
        b = block(me2 + 1, 2, 2)
        far_m = send(b, b, ax2(3))
        b = block(me2 + 1)
        copy(b, b, twin, k).start()
        yield
        far_p.wait_recv()
        far_m.wait_recv()
        b = block(me2 + 2)
        copy(b, b, twin, k).start()
        sent.append(tw)
        yield
        tw.wait_recv()
        yield

    def gather_z():
        own = WC.at[z, c, y]
        k, row = group(own)
        trio = WC.at[0, 0, pl.ds(0, 3)]

        def start_row():
            for d in (1, 2, 3):
                copy(own, own, at_x(d), k).start()

        pl.when(source)(start_row)
        yield
        pl.when(jnp.logical_not(source))(row.wait_recv)
        col = send_group(trio, [(own, own, at_y(d)) for d in (2, 1, 3)])
        yield
        col.wait_recv()

        def block(d, lo=0, n=4):
            return WC.at[(z + d) % 8, c, pl.ds(lo, n)]

        b = block(0)
        up, down = send(b, b, at_z(1)), send(b, b, at_z(7))
        kt, tw = group(WC.at[:, 0])
        copy(b, b, twin, kt).start()
        yield
        for step in (1, 2, 3):
            n = 2 if step == 3 else 4
            up.wait_recv()
            b = block(8 - step, 0, n)
            up = send(b, b, at_z(1))
            down.wait_recv()
            b = block(step, 4 - n, n)
            down = send(b, b, at_z(7))
            for d in (8 - step, step):
                b = block(d)
                copy(b, b, twin, kt).start()
            yield
        up.wait_recv()
        down.wait_recv()
        b = block(4)
        copy(b, b, twin, kt).start()
        sent.append(tw)
        yield
        tw.wait_recv()
        pl.when(source)(copy(trio, trio, twin, k).wait_send)
        yield

    def scatter(h):
        if h == 0:
            me1, me2, ax1, ax2 = x, y, at_x, at_y
        else:
            me1, me2, ax1, ax2 = y, x, at_y, at_x

        def piece(buf, a, s, b):
            return buf.at[a % 4, s, b % 4, 0] if h == 0 else buf.at[b % 4, s, a % 4, 1]

        turn = (2, 1, 3, 0)
        far, near, both = {}, {}, {}

        def send_far(p):
            far[p] = [
                send_group(
                    R2.at[h, j, pl.ds(2 * p, 2)],
                    [(piece(Gs, me1 + 2, j, me2 + turn[q]), R2.at[h, j, q], to) for q in (2 * p, 2 * p + 1)],
                )
                for j, to in enumerate((ax1(1), ax1(3)))
            ]

        def send_near(p):
            near[p] = [
                send_group(
                    R1.at[h, j, 1 - j, pl.ds(2 * p, 2)],
                    [(piece(Gs, a, 1 - j, me2 + turn[q]), R1.at[h, j, 1 - j, q], to) for q in (2 * p, 2 * p + 1)],
                )
                for j, (a, to) in enumerate(((me1 + 1, ax1(1)), (me1 + 3, ax1(3))))
            ]

        def send_both(p):
            both[p] = []
            for j, (a, to) in enumerate(((me1 + 1, ax1(1)), (me1 + 3, ax1(3)))):
                far[p][j].wait_recv()
                copies = []
                for q in (2 * p, 2 * p + 1):
                    b = me2 + turn[q]
                    r = piece(Gs, a, j, b)
                    r[...] = (piece(G, a, j, b)[...] + R2[h, j, q].astype(F32)).astype(BF16)
                    copies.append((r, R1.at[h, j, j, q], to))
                both[p].append(send_group(R1.at[h, j, j, pl.ds(2 * p, 2)], copies))

        def arrived(p):
            for cp in (*near[p], *both[p]):
                cp.wait_recv()

        def total(q):
            b = me2 + turn[q]
            for s in range(2):
                g = piece(G, me1, s, b)
                v = g[...] + R1[h, 0, s, q].astype(F32) + R1[h, 1, s, q].astype(F32)
                g[...] = v
                piece(Gs, me1, s, b)[...] = v.astype(BF16)

        def two(buf, q, s):
            return piece(buf, me1, s, me2 + turn[q])

        send_far(0)
        yield
        send_far(1)
        yield
        send_near(0)
        yield
        send_both(0)
        yield
        send_near(1)
        yield
        send_both(1)
        yield
        arrived(0)
        total(0)
        far_p = send(two(Gs, 0, 0), Q2.at[h, 0], ax2(1))
        far_m = send(two(Gs, 0, 1), Q2.at[h, 1], ax2(3))
        total(1)
        near_p = send(two(Gs, 1, 1), Q1.at[h, 0, 1], ax2(1))
        yield
        far_p.wait_recv()
        two(Gs, 1, 0)[...] = (two(G, 1, 0)[...] + Q2[h, 0].astype(F32)).astype(BF16)
        both_p = send(two(Gs, 1, 0), Q1.at[h, 0, 0], ax2(1))
        yield
        arrived(1)
        total(2)
        near_m = send(two(Gs, 2, 0), Q1.at[h, 1, 0], ax2(3))
        far_m.wait_recv()
        two(Gs, 2, 1)[...] = (two(G, 2, 1)[...] + Q2[h, 1].astype(F32)).astype(BF16)
        both_m = send(two(Gs, 2, 1), Q1.at[h, 1, 1], ax2(3))
        total(3)
        yield
        for cp in (near_p, near_m, both_p, both_m):
            cp.wait_recv()
        away = 1 - zh
        two(Gs, 3, away)[...] = (
            two(G, 3, away)[...] + Q1[h, 0, away].astype(F32) + Q1[h, 1, away].astype(F32)
        ).astype(BF16)
        last = send(two(Gs, 3, away), Z3.at[h], at_z(4))
        yield
        mine = two(G, 3, zh)[...] + Q1[h, 0, zh].astype(F32) + Q1[h, 1, zh].astype(F32)
        last.wait_recv()
        res[pl.ds(16 * h, 16), :] = mine + Z3[h].astype(F32)
        yield

    def allreduce(k):
        cp = send(T.at[k, 1 - c], RC.at[k], twin)
        yield
        cp.wait_recv()
        A1[k] = T[k, c] + RC[k]
        got = send_group(
            RP.at[k],
            [
                (A1.at[k, (x + dx) % 4, (y + dy) % 4], RP.at[k, e], at_xy(dx, dy))
                for e, (dx, dy) in enumerate(plane)
            ],
        )
        yield
        got.wait_recv()
        v = A1[k, x, y]
        for e in range(len(plane)):
            v = v + RP[k, e]
        mine = RZ.at[k, z]
        mine[...] = v
        got = send_group(RZ.at[k, pl.ds(0, 7)], [(mine, mine, at_z(d)) for d in (4, 3, 5, 2, 6, 1, 7)])
        yield
        got.wait_recv()
        v = ((RZ[k, 0] + RZ[k, 1]) + (RZ[k, 2] + RZ[k, 3])) + ((RZ[k, 4] + RZ[k, 5]) + (RZ[k, 6] + RZ[k, 7]))
        mine = F.at[k, c * 4 + x, y]
        mine[...] = v
        got = send_group(RP.at[k], [(mine, mine, at_xy(*p)) for p in plane])
        yield
        got.wait_recv()
        half = F.at[k, pl.ds(c * 4, 4)]
        cp = send(half, half, twin)
        yield
        cp.wait_recv()
        yield

    def full(k):
        return jnp.concatenate([F[k, :, j].reshape(R, 512) for j in range(4)], axis=1)

    def put(k, v):
        for a in range(8):
            for j in range(4):
                T[k, a // 4, a % 4, j] = v[8 * a : 8 * (a + 1), 512 * j : 512 * (j + 1)]

    def my_rows(k):
        v = F[k, :, i // 16].reshape(R, 512)
        for n in (128, 32):
            place = (i // (n // 32)) % 4
            blk = v[:, :n]
            for j in range(1, 4):
                blk = jnp.where(place == j, v[:, n * j : n * (j + 1)], blk)
            v = blk
        return v

    own_w = [gather(True, h) for h in range(2)]
    oth_w = [gather(False, h) for h in range(2)]
    z_w = gather_z()
    grads = [scatter(h) for h in range(2)]
    red = [allreduce(k) for k in range(2)]

    def adv(*gens):
        for g in gens:
            next(g)

    def transpose_acts():
        for b in range(8):
            t = acts[:, 256 * b : 256 * (b + 1)].T
            for j in range(8):
                AT[j % 2, j // 2, pl.ds(32 * b, 32)] = t[32 * j : 32 * (j + 1)]

    def left_factor():
        basis_t = basis[...]
        b3 = split3(basis_t)
        u = fold3(nt(b3, go[...]))
        al.wait()
        p = fold3(nn(split3(u), acts[...]))
        el.wait()
        eb = jnp.concatenate([nt(basis_t, err[...], HI)] * 4, axis=1)
        col = lax.broadcasted_iota(jnp.int32, (R, D), 1)
        eb = jnp.where(col // 32 == i, jnp.concatenate([eb] * 16, axis=1), 0.0)
        put(0, (p * scale + eb) * (1.0 / GROUPS))

    def right_factor():
        pt = full(0)
        v = fold3(nt(split3(pt), acts[...]))
        s = fold3(nn(split3(v), go[...]))
        pe = nn(my_rows(0), err[...], HI)
        put(1, (s * scale + pe) * (1.0 / GROUPS))

    def gram():
        pt = full(0)
        row = lax.broadcasted_iota(jnp.int32, (R, R), 0)
        col = lax.broadcasted_iota(jnp.int32, (R, R), 1)
        M[...] = jnp.concatenate([nt(pt, pt, HI), (row == col).astype(F32)], axis=1)

    def factor(lo, hi):
        row = lax.broadcasted_iota(jnp.int32, (R, 2 * R), 0)
        col = lax.broadcasted_iota(jnp.int32, (R, 2 * R), 1)

        def body(k, m):
            rk = jnp.sum(jnp.where(row == k, m, 0.0), axis=0, keepdims=True)
            ck = jnp.sum(jnp.where(col == k, m, 0.0), axis=1, keepdims=True)
            piv = jnp.sum(jnp.where(col[:1] == k, rk, 0.0), axis=1, keepdims=True)
            rk = rk / jnp.sqrt(piv)
            ck = ck / jnp.sqrt(piv)
            return jnp.where(row > k, m - ck * rk, jnp.where(row == k, rk, m))

        M[...] = lax.fori_loop(lo, hi, body, M[...])

    def grad_own(d):
        a = (x + d) % 4

        def body(n, carry):
            cols = pl.ds(pl.multiple_of(n * 512, 512), 512)
            v = nn(AT[c, a], go[:, cols])
            G[a, :, :, :, :, cols] = v.reshape(2, 4, 2, 16, 512)
            return carry

        lax.fori_loop(0, 4, body, 0)

    def grad_twin(d):
        a = (x + d) % 4

        def body(n, carry):
            cols = pl.ds(pl.multiple_of(n * 512, 512), 512)
            v = nn(RT[a], go_tw[:, cols]).reshape(2, 4, 2, 16, 512)
            v = (v + G[a, :, :, :, :, cols]) * scale
            G[a, :, :, :, :, cols] = v
            Gs[a, :, :, :, :, cols] = v.astype(BF16)
            return carry

        lax.fori_loop(0, 4, body, 0)

    def grad_acts(*blocks):
        for j in blocks:
            s, b = j // 4, j % 4
            w = jnp.concatenate(
                [v for a in range(4) for k in range(2) for v in (WA[s, b, a, k], WC[s * 4 + (a + b) % 4, k, b])], axis=0
            )
            ga[:, 256 * j : 256 * (j + 1)] = nt(go[...], w).astype(BF16)

    def drain():
        while sent:
            sent.pop(0).wait_send()

    bl.wait()
    gl.wait()
    left_factor()
    wl[0].wait()
    pl.when(source)(wl[1].wait)
    pl.semaphore_wait(barrier, len(peers))
    adv(red[0])
    adv(*own_w)
    wz = send(WA.at[zh, y, x, c], WA.at[zh, y, x, c], mirror)
    adv(z_w)
    got = send(go, go_tw, twin)
    transpose_acts()
    att = send(AT.at[1 - c], RT, twin)
    grad_own(2)
    adv(red[0])
    grad_own(1)
    adv(*own_w)
    adv(z_w)
    grad_own(3)
    grad_own(0)
    adv(*own_w)
    wz.wait_recv()
    adv(*oth_w)
    adv(red[0])
    adv(z_w)
    got.wait_recv()
    att.wait_recv()
    grad_twin(2)
    adv(*own_w)
    grad_twin(1)
    adv(red[0])
    adv(grads[0])
    adv(grads[0])
    grad_twin(3)
    adv(grads[0])
    grad_twin(0)
    adv(grads[1])
    adv(grads[1])
    adv(grads[1])
    adv(*oth_w)
    adv(z_w)
    adv(red[0])
    adv(*own_w)
    adv(grads[0])
    adv(red[0])
    right_factor()
    adv(red[1])
    adv(grads[1])
    gram()
    adv(red[1])
    adv(*grads)
    factor(0, 16)
    adv(z_w)
    adv(*grads)
    factor(16, 32)
    adv(red[1])
    adv(*oth_w)
    adv(*grads)
    factor(32, 64)
    adv(red[1])
    ortho = nn(M[:, R:], my_rows(0), HI).T
    adv(z_w)
    adv(*grads)
    adv(*oth_w)
    adv(*own_w)
    adv(*grads)
    adv(z_w)
    adv(*oth_w)
    adv(red[1])
    adv(*grads)
    adv(z_w)
    adv(*oth_w)
    grad_acts(0, 1)
    adv(red[1])
    qf = nn(M[:, R:], full(1), HI)
    qt[...] = qf
    ap = nn(ortho, qf, HI)
    apv[...] = ap
    grad_acts(2, 3, 4, 5, 6, 7)
    adv(*grads)
    res[...] = res[...] + err[...] - ap
    drain()
    assert count[0] <= SEMS, count[0]
    for g in own_w + oth_w + [z_w] + grads + red:
        assert next(g, 0) == 0


def write_out(a, b, c, d, ao, bo, co, do, sem):
    cps = [pltpu.make_async_copy(v, o, sem.at[k]) for k, (v, o) in enumerate(((a, ao), (b, bo), (c, co), (d, do)))]
    for cp in cps:
        cp.start()
    for cp in cps:
        cp.wait()


def shards(acts, grad_out, weight, error, basis):
    scale = 1.0 / math.sqrt(TOK * lax.axis_size("inner"))
    hbm = pl.BlockSpec(memory_space=pltpu.HBM)
    vm = pltpu.VMEM
    ga, approx, err, qt = pl.pallas_call(
        functools.partial(kernel, scale),
        out_shape=(vm((TOK, D), BF16), vm((32, D), F32), vm((32, D), F32), vm((R, D), F32)),
        in_specs=[hbm] * 5,
        out_specs=(pl.BlockSpec(memory_space=vm),) * 4,
        scratch_shapes=[
            vm((TOK, D), BF16),
            vm((TOK, D), BF16),
            vm((32, D), F32),
            vm((R, D), F32),
            vm((2, 4, 4, 2, 16, D), BF16),
            vm((8, 2, 4, 16, D), BF16),
            vm((2, 4, 256, TOK), BF16),
            vm((4, 256, TOK), BF16),
            vm((TOK, D), BF16),
            vm((4, 2, 4, 2, 16, D), F32),
            vm((4, 2, 4, 2, 16, D), BF16),
            vm((2, 2, 2, 4, 16, D), BF16),
            vm((2, 2, 4, 16, D), BF16),
            vm((2, 2, 2, 16, D), BF16),
            vm((2, 2, 16, D), BF16),
            vm((2, 16, D), BF16),
            vm((2, 2, 4, 4, 8, 512), F32),
            vm((2, 4, 4, 8, 512), F32),
            vm((2, 4, 4, 8, 512), F32),
            vm((2, 15, 8, 512), F32),
            vm((2, 8, 8, 512), F32),
            vm((2, 8, 4, 8, 512), F32),
            vm((R, 2 * R), F32),
            pltpu.SemaphoreType.DMA((6,)),
            pltpu.SemaphoreType.DMA((SEMS,)),
            pltpu.SemaphoreType.DMA((SEMS,)),
        ],
        compiler_params=pltpu.CompilerParams(
            collective_id=0, has_side_effects=True, vmem_limit_bytes=60 * 2**20
        ),
        name="powersgd",
    )(acts, grad_out, weight, error[0], basis.T)
    ga, approx, err, qt = pl.pallas_call(
        write_out,
        out_shape=(
            jax.ShapeDtypeStruct((TOK, D), BF16),
            jax.ShapeDtypeStruct((32, D), F32),
            jax.ShapeDtypeStruct((32, D), F32),
            jax.ShapeDtypeStruct((R, D), F32),
        ),
        in_specs=[pl.BlockSpec(memory_space=pl.ANY)] * 4,
        out_specs=(hbm,) * 4,
        scratch_shapes=[pltpu.SemaphoreType.DMA((4,))],
        compiler_params=pltpu.CompilerParams(vmem_limit_bytes=2**20),
        name="write_out",
    )(ga, approx, err, qt)
    return (ga, approx, err[None], qt.T)


def solution(mesh):
    in_specs = (
        P(("inner", "outer"), None),
        P(("inner", "outer"), None),
        P("inner", None),
        P("outer", "inner", None),
        P(),
    )
    out_specs = (P(("inner", "outer"), None), P("inner", None), P("outer", "inner", None), P())
    return jax.shard_map(shards, mesh=mesh, in_specs=in_specs, out_specs=out_specs, check_vma=False)
```

time: 109 us -> 75.8 us (0.70)
  Pallas kernels: 101 us -> 74.7 us
  local copies, waits for them, and re-layouts: 7.81 us -> 0 us
    pallas_call x1 -> x2, Pallas kernels: 101 us -> 74.7 us  [the longest x1 73 us: shards(): pl.pallas_call(functools.partial(kernel, scale), out_shape=(vm((TOK, D),...]
    unnamed x11 -> x0, local copies, waits for them, and re-layouts: 7.81 us -> none
where the time goes in v2:
time: 75.8 us; the launch traced here: 75.5 us
  Pallas kernels  74.7 us (99%)
  between operations  0.8 us (1%)
    pallas_call x1, Pallas kernels, shards(): pl.pallas_call(functools.partial(kernel, scale), out_shape=(vm((TOK, D),...  73 us
    pallas_call x1, Pallas kernels, shards(): pl.pallas_call(write_out, out_shape=(jax.ShapeDtypeStruct((TOK, D), BF16)...  1.69 us

profile of v2, /device:TPU:1, one launch (start us, length us, event | category | flops | bytes accessed | tf_op | source)
XLA Modules:
  0.0 75.5 jit_solution(6008753706015648147)
XLA Ops:
  0.6 73.0 %powersgd.1 = (bf16[512,2048]{1,0:T(8,128)(2,1)S(1)}, f32[32,2048]{1,0:T(8,128)S(1)}, f32[32,2048]{1,0:T(8,128)S(1)}, f32[64,2048]{1,0:T(8,128)S(1)}) custom-call(bf16[512,2048]{1,0:T(8,128)(2,1)} %acts_hbm.1, bf16[512,2048]{1,0:T(8,128)(2,1)} %go_hbm.1, bf16[32,2048]{1,0:T(8,128)(2,1)} %weight_hbm.1, f32[32,2048]{1,0:T(8,128)} %bitcast.5, f32[64,2048]{1,0:T(8,128)} %bitcast.4), custom_call_target="tpu_custom_call" | custom-call | tf_op jit(solution)/shard_map/powersgd/pallas_call | solution.py:568
  73.6 1.7 %write_out.1 = (bf16[512,2048]{1,0:T(8,128)(2,1)}, f32[32,2048]{1,0:T(8,128)}, f32[32,2048]{1,0:T(8,128)}, f32[64,2048]{1,0:T(8,128)}) custom-call(bf16[512,2048]{1,0:T(8,128)(2,1)S(1)} %get-tuple-element.12.a, f32[32,2048]{1,0:T(8,128)S(1)} %get-tuple-element.13.b, f32[32,2048]{1,0:T(8,128)S(1)} %get-tuple-element.14.c, f32[64,2048]{1,0:T(8,128)S(1)} %get-tuple-element.15.d), custom_call_target="tpu_custom_call" | custom-call | tf_op jit(solution)/shard_map/write_out/pallas_call | solution.py:606

commit v3 on v2

--- a/solution.py
+++ b/solution.py
@@ -17,7 +17,7 @@
 D = 2048
 R = 64
 GROUPS = 4
-SEMS = 96
+SEMS = 94
 
 
 def nn(a, b, precision=None):
@@ -45,7 +45,7 @@
     acts_hbm, go_hbm, weight_hbm, error_hbm, basis_hbm,
     ga, apv, res, qt,
     acts, go, err, basis, WA, WC, AT, RT, go_tw, G, Gs, R1, R2, Q1, Q2, Z3,
-    T, RC, A1, RP, RZ, F, M,
+    T, RC, A1, RP, RP2, RZ, F, M,
     lsem, ssem, rsem,
 ):
     i = lax.axis_index("inner")
@@ -116,7 +116,7 @@
     el = pltpu.make_async_copy(error_hbm, err, lsem.at[5])
     wl[0].start()
     pl.when(source)(wl[1].start)
-    for cp in (bl, gl, al, el):
+    for cp in (bl, el, gl, al):
         cp.start()
 
     barrier = pltpu.get_barrier_semaphore()
@@ -327,7 +327,8 @@
         cp = send(T.at[k, 1 - c], RC.at[k], twin)
         yield
         cp.wait_recv()
-        A1[k] = T[k, c] + RC[k]
+        v = T[k, c] + RC[k]
+        A1[k] = jnp.concatenate([v[..., :256], v[..., 256:]], axis=2).astype(BF16)
         got = send_group(
             RP.at[k],
             [
@@ -337,9 +338,10 @@
         )
         yield
         got.wait_recv()
-        v = A1[k, x, y]
-        for e in range(len(plane)):
-            v = v + RP[k, e]
+        v = RP[k, 0].astype(F32)
+        for e in range(1, len(plane)):
+            v = v + RP[k, e].astype(F32)
+        v = T[k, c, x, y] + RC[k, x, y] + jnp.concatenate([v[:8], v[8:]], axis=1)
         mine = RZ.at[k, z]
         mine[...] = v
         got = send_group(RZ.at[k, pl.ds(0, 7)], [(mine, mine, at_z(d)) for d in (4, 3, 5, 2, 6, 1, 7)])
@@ -348,7 +350,7 @@
         v = ((RZ[k, 0] + RZ[k, 1]) + (RZ[k, 2] + RZ[k, 3])) + ((RZ[k, 4] + RZ[k, 5]) + (RZ[k, 6] + RZ[k, 7]))
         mine = F.at[k, c * 4 + x, y]
         mine[...] = v
-        got = send_group(RP.at[k], [(mine, mine, at_xy(*p)) for p in plane])
+        got = send_group(RP2, [(mine, mine, at_xy(*p)) for p in plane])
         yield
         got.wait_recv()
         half = F.at[k, pl.ds(c * 4, 4)]
@@ -391,16 +393,15 @@
             for j in range(8):
                 AT[j % 2, j // 2, pl.ds(32 * b, 32)] = t[32 * j : 32 * (j + 1)]
 
-    def left_factor():
-        basis_t = basis[...]
-        b3 = split3(basis_t)
-        u = fold3(nt(b3, go[...]))
+    def error_term():
+        eb = jnp.concatenate([nt(basis[...], err[...], HI)] * 4, axis=1)
+        col = lax.broadcasted_iota(jnp.int32, (R, D), 1)
+        return jnp.where(col // 32 == i, jnp.concatenate([eb] * 16, axis=1), 0.0)
+
+    def left_factor(eb):
+        u = fold3(nt(split3(basis[...]), go[...]))
         al.wait()
         p = fold3(nn(split3(u), acts[...]))
-        el.wait()
-        eb = jnp.concatenate([nt(basis_t, err[...], HI)] * 4, axis=1)
-        col = lax.broadcasted_iota(jnp.int32, (R, D), 1)
-        eb = jnp.where(col // 32 == i, jnp.concatenate([eb] * 16, axis=1), 0.0)
         put(0, (p * scale + eb) * (1.0 / GROUPS))
 
     def right_factor():
@@ -454,97 +455,102 @@
 
         lax.fori_loop(0, 4, body, 0)
 
-    def grad_acts(*blocks):
-        for j in blocks:
-            s, b = j // 4, j % 4
+    def grad_acts(s, *blocks):
+        for b in blocks:
             w = jnp.concatenate(
                 [v for a in range(4) for k in range(2) for v in (WA[s, b, a, k], WC[s * 4 + (a + b) % 4, k, b])], axis=0
             )
-            ga[:, 256 * j : 256 * (j + 1)] = nt(go[...], w).astype(BF16)
+            cols = pl.ds(pl.multiple_of((s * 4 + b) * 256, 256), 256)
+            ga[:, cols] = nt(go[...], w).astype(BF16)
 
     def drain():
         while sent:
             sent.pop(0).wait_send()
 
+    wl[0].wait()
     bl.wait()
-    gl.wait()
-    left_factor()
-    wl[0].wait()
+    el.wait()
+    eb = error_term()
     pl.when(source)(wl[1].wait)
     pl.semaphore_wait(barrier, len(peers))
+    adv(*own_w)
+    wz = send(WA.at[zh, y, x, c], WA.at[zh, y, x, c], mirror)
+    adv(z_w)
+    gl.wait()
+    left_factor(eb)
+    adv(red[0])
+    got = [send(go, go_tw, twin)]
+    transpose_acts()
+    got.append(send(AT.at[1 - c], RT, twin))
     adv(red[0])
     adv(*own_w)
-    wz = send(WA.at[zh, y, x, c], WA.at[zh, y, x, c], mirror)
-    adv(z_w)
-    got = send(go, go_tw, twin)
-    transpose_acts()
-    att = send(AT.at[1 - c], RT, twin)
+    adv(z_w)
     grad_own(2)
-    adv(red[0])
     grad_own(1)
-    adv(*own_w)
-    adv(z_w)
+    wz.wait_recv()
+    adv(*oth_w)
     grad_own(3)
     grad_own(0)
+    adv(red[0])
     adv(*own_w)
-    wz.wait_recv()
+    adv(z_w)
     adv(*oth_w)
-    adv(red[0])
-    adv(z_w)
-    got.wait_recv()
-    att.wait_recv()
+    for cp in got:
+        cp.wait_recv()
     grad_twin(2)
     adv(*own_w)
-    grad_twin(1)
     adv(red[0])
     adv(grads[0])
     adv(grads[0])
+    grad_twin(1)
     grad_twin(3)
     adv(grads[0])
     grad_twin(0)
     adv(grads[1])
     adv(grads[1])
     adv(grads[1])
-    adv(*oth_w)
     adv(z_w)
     adv(red[0])
-    adv(*own_w)
-    adv(grads[0])
     adv(red[0])
     right_factor()
     adv(red[1])
-    adv(grads[1])
+    adv(grads[0])
     gram()
     adv(red[1])
+    adv(grads[1])
     adv(*grads)
     factor(0, 16)
     adv(z_w)
     adv(*grads)
+    adv(*oth_w)
     factor(16, 32)
     adv(red[1])
-    adv(*oth_w)
     adv(*grads)
-    factor(32, 64)
+    adv(*own_w)
+    factor(32, 48)
+    adv(*own_w)
+    adv(z_w)
+    factor(48, 64)
     adv(red[1])
     ortho = nn(M[:, R:], my_rows(0), HI).T
-    adv(z_w)
+    adv(*grads)
+    adv(z_w)
+    adv(*grads)
+    adv(z_w)
+    grad_acts(zh, 0)
+    adv(red[1])
     adv(*grads)
     adv(*oth_w)
-    adv(*own_w)
-    adv(*grads)
-    adv(z_w)
-    adv(*oth_w)
-    adv(red[1])
-    adv(*grads)
-    adv(z_w)
-    adv(*oth_w)
-    grad_acts(0, 1)
+    grad_acts(zh, 1)
     adv(red[1])
     qf = nn(M[:, R:], full(1), HI)
     qt[...] = qf
     ap = nn(ortho, qf, HI)
     apv[...] = ap
-    grad_acts(2, 3, 4, 5, 6, 7)
+    adv(*oth_w)
+    grad_acts(zh, 2, 3)
+    adv(*oth_w)
+    grad_acts(1 - zh, 0, 1, 2, 3)
     adv(*grads)
     res[...] = res[...] + err[...] - ap
     drain()
@@ -589,8 +595,9 @@
             vm((2, 16, D), BF16),
             vm((2, 2, 4, 4, 8, 512), F32),
             vm((2, 4, 4, 8, 512), F32),
-            vm((2, 4, 4, 8, 512), F32),
-            vm((2, 15, 8, 512), F32),
+            vm((2, 4, 4, 16, 256), BF16),
+            vm((2, 15, 16, 256), BF16),
+            vm((15, 8, 512), F32),
             vm((2, 8, 8, 512), F32),
             vm((2, 8, 4, 8, 512), F32),
             vm((R, 2 * R), F32),

time: 75.8 us -> 73.1 us (0.964)
  Pallas kernels: 74.7 us -> 72.2 us
    pallas_call x1, Pallas kernels: 73 us -> 70.5 us  [shards(): pl.pallas_call(functools.partial(kernel, scale), out_shape=(vm((TOK, D),...]
where the time goes in v3:
time: 73.1 us; the launch traced here: 73 us
  Pallas kernels  72.2 us (99%)
  between operations  0.8 us (1%)
    pallas_call x1, Pallas kernels, shards(): pl.pallas_call(functools.partial(kernel, scale), out_shape=(vm((TOK, D),...  70.5 us
    pallas_call x1, Pallas kernels, shards(): pl.pallas_call(write_out, out_shape=(jax.ShapeDtypeStruct((TOK, D), BF16)...  1.69 us

profile of v3, /device:TPU:1, one launch (start us, length us, event | category | flops | bytes accessed | tf_op | source)
XLA Modules:
  0.0 73.0 jit_solution(4714695820654569012)
XLA Ops:
  0.6 70.5 %powersgd.1 = (bf16[512,2048]{1,0:T(8,128)(2,1)S(1)}, f32[32,2048]{1,0:T(8,128)S(1)}, f32[32,2048]{1,0:T(8,128)S(1)}, f32[64,2048]{1,0:T(8,128)S(1)}) custom-call(bf16[512,2048]{1,0:T(8,128)(2,1)} %acts_hbm.1, bf16[512,2048]{1,0:T(8,128)(2,1)} %go_hbm.1, bf16[32,2048]{1,0:T(8,128)(2,1)} %weight_hbm.1, f32[32,2048]{1,0:T(8,128)} %bitcast.5, f32[64,2048]{1,0:T(8,128)} %bitcast.4), custom_call_target="tpu_custom_call" | custom-call | tf_op jit(solution)/shard_map/powersgd/pallas_call | solution.py:574
  71.1 1.7 %write_out.1 = (bf16[512,2048]{1,0:T(8,128)(2,1)}, f32[32,2048]{1,0:T(8,128)}, f32[32,2048]{1,0:T(8,128)}, f32[64,2048]{1,0:T(8,128)}) custom-call(bf16[512,2048]{1,0:T(8,128)(2,1)S(1)} %get-tuple-element.12.a, f32[32,2048]{1,0:T(8,128)S(1)} %get-tuple-element.13.b, f32[32,2048]{1,0:T(8,128)S(1)} %get-tuple-element.14.c, f32[64,2048]{1,0:T(8,128)S(1)} %get-tuple-element.15.d), custom_call_target="tpu_custom_call" | custom-call | tf_op jit(solution)/shard_map/write_out/pallas_call | solution.py:613

commit v4 on v3

--- a/solution.py
+++ b/solution.py
@@ -17,7 +17,8 @@
 D = 2048
 R = 64
 GROUPS = 4
-SEMS = 94
+RECV = 94
+SEND = 27
 
 
 def nn(a, b, precision=None):
@@ -76,33 +77,36 @@
         key=lambda p: -(min(p[0], 4 - p[0]) + min(p[1], 4 - p[1])),
     )
 
-    count = [0]
+    count = [0, 0]
     sent = []
 
-    def copy(src, dst, to, k=None):
-        if k is None:
-            k = count[0]
-            count[0] += 1
+    def take(j):
+        count[j] += 1
+        return count[j] - 1
+
+    def copy(src, dst, to, k, ks):
         return pltpu.make_async_remote_copy(
-            src_ref=src, dst_ref=dst, send_sem=ssem.at[k], recv_sem=rsem.at[k], device_id=to, device_id_type=MESH
+            src_ref=src, dst_ref=dst, send_sem=ssem.at[ks], recv_sem=rsem.at[k], device_id=to, device_id_type=MESH
         )
 
-    def send(src, dst, to):
-        cp = copy(src, dst, to)
+    def together(size):
+        ks = take(1)
+        sent.append(copy(size, size, twin, 0, ks))
+        return ks
+
+    def send(src, dst, to, ks=None):
+        cp = copy(src, dst, to, take(0), together(src) if ks is None else ks)
         cp.start()
-        sent.append(cp)
         return cp
 
-    def group(size):
-        k = count[0]
-        count[0] += 1
-        return k, copy(size, size, twin, k)
-
-    def send_group(size, copies):
-        k, whole = group(size)
-        for src, dst, to in copies:
-            copy(src, dst, to, k).start()
-        sent.append(whole)
+    def group(size, ks=None):
+        k, ks = take(0), together(size) if ks is None else ks
+        return copy(size, size, twin, k, ks), lambda src, dst, to: copy(src, dst, to, k, ks).start()
+
+    def send_group(size, copies, ks=None):
+        whole, start = group(size, ks)
+        for c3 in copies:
+            start(*c3)
         return whole
 
     source = (x + y) % 4 == zl
@@ -140,50 +144,52 @@
                 return WA.at[zs, b % 4, pl.ds(lo, n), c, :, cols]
             return WA.at[zs, pl.ds(lo, n), b % 4, c, :, cols]
 
+        ks = together(WA.at[0, 0, pl.ds(0, 3), 0, :, cols])
         p = piece(me1)
-        up = send(p, p, ax1(1))
-        down = send(p, p, ax1(3))
+        up = send(p, p, ax1(1), ks)
+        down = send(p, p, ax1(3), ks)
         yield
         up.wait_recv()
         p = piece(me1 + 3)
-        far = send(p, p, ax1(1))
+        far = send(p, p, ax1(1), ks)
         down.wait_recv()
         yield
         far.wait_recv()
+        ks = together(go_tw.at[pl.ds(0, 224)])
         b = block(me2)
-        up = send(b, b, ax2(1))
-        down = send(b, b, ax2(3))
-        k, tw = group(WA.at[0, :, :, 0, :, cols])
-        copy(b, b, twin, k).start()
+        up = send(b, b, ax2(1), ks)
+        down = send(b, b, ax2(3), ks)
+        tw, to_twin = group(WA.at[0, :, :, 0, :, cols], ks)
+        to_twin(b, b, twin)
         yield
         up.wait_recv()
         b = block(me2 + 3, 0, 2)
-        far_p = send(b, b, ax2(1))
+        far_p = send(b, b, ax2(1), ks)
         b = block(me2 + 3)
-        copy(b, b, twin, k).start()
+        to_twin(b, b, twin)
         down.wait_recv()
         b = block(me2 + 1, 2, 2)
-        far_m = send(b, b, ax2(3))
+        far_m = send(b, b, ax2(3), ks)
         b = block(me2 + 1)
-        copy(b, b, twin, k).start()
+        to_twin(b, b, twin)
         yield
         far_p.wait_recv()
         far_m.wait_recv()
         b = block(me2 + 2)
-        copy(b, b, twin, k).start()
-        sent.append(tw)
+        to_twin(b, b, twin)
         yield
         tw.wait_recv()
         yield
 
     def gather_z():
         own = WC.at[z, c, y]
-        k, row = group(own)
+        row_ks = take(1)
+        row, to_row = group(own, row_ks)
         trio = WC.at[0, 0, pl.ds(0, 3)]
 
         def start_row():
             for d in (1, 2, 3):
-                copy(own, own, at_x(d), k).start()
+                to_row(own, own, at_x(d))
 
         pl.when(source)(start_row)
         yield
@@ -196,30 +202,30 @@
             return WC.at[(z + d) % 8, c, pl.ds(lo, n)]
 
         b = block(0)
-        up, down = send(b, b, at_z(1)), send(b, b, at_z(7))
-        kt, tw = group(WC.at[:, 0])
-        copy(b, b, twin, kt).start()
+        ks = together(go_tw.at[pl.ds(0, 448)])
+        up, down = send(b, b, at_z(1), ks), send(b, b, at_z(7), ks)
+        tw, to_twin = group(WC.at[:, 0])
+        to_twin(b, b, twin)
         yield
         for step in (1, 2, 3):
             n = 2 if step == 3 else 4
             up.wait_recv()
             b = block(8 - step, 0, n)
-            up = send(b, b, at_z(1))
+            up = send(b, b, at_z(1), ks)
             down.wait_recv()
             b = block(step, 4 - n, n)
-            down = send(b, b, at_z(7))
+            down = send(b, b, at_z(7), ks)
             for d in (8 - step, step):
                 b = block(d)
-                copy(b, b, twin, kt).start()
+                to_twin(b, b, twin)
             yield
         up.wait_recv()
         down.wait_recv()
         b = block(4)
-        copy(b, b, twin, kt).start()
-        sent.append(tw)
+        to_twin(b, b, twin)
         yield
         tw.wait_recv()
-        pl.when(source)(copy(trio, trio, twin, k).wait_send)
+        pl.when(source)(copy(trio, trio, twin, 0, row_ks).wait_send)
         yield
 
     def scatter(h):
@@ -231,6 +237,7 @@
         def piece(buf, a, s, b):
             return buf.at[a % 4, s, b % 4, 0] if h == 0 else buf.at[b % 4, s, a % 4, 1]
 
+        ks = together(go_tw.at[pl.ds(0, 496)])
         turn = (2, 1, 3, 0)
         far, near, both = {}, {}, {}
 
@@ -239,6 +246,7 @@
                 send_group(
                     R2.at[h, j, pl.ds(2 * p, 2)],
                     [(piece(Gs, me1 + 2, j, me2 + turn[q]), R2.at[h, j, q], to) for q in (2 * p, 2 * p + 1)],
+                    ks,
                 )
                 for j, to in enumerate((ax1(1), ax1(3)))
             ]
@@ -248,6 +256,7 @@
                 send_group(
                     R1.at[h, j, 1 - j, pl.ds(2 * p, 2)],
                     [(piece(Gs, a, 1 - j, me2 + turn[q]), R1.at[h, j, 1 - j, q], to) for q in (2 * p, 2 * p + 1)],
+                    ks,
                 )
                 for j, (a, to) in enumerate(((me1 + 1, ax1(1)), (me1 + 3, ax1(3))))
             ]
@@ -262,7 +271,7 @@
                     r = piece(Gs, a, j, b)
                     r[...] = (piece(G, a, j, b)[...] + R2[h, j, q].astype(F32)).astype(BF16)
                     copies.append((r, R1.at[h, j, j, q], to))
-                both[p].append(send_group(R1.at[h, j, j, pl.ds(2 * p, 2)], copies))
+                both[p].append(send_group(R1.at[h, j, j, pl.ds(2 * p, 2)], copies, ks))
 
         def arrived(p):
             for cp in (*near[p], *both[p]):
@@ -293,21 +302,21 @@
         yield
         arrived(0)
         total(0)
-        far_p = send(two(Gs, 0, 0), Q2.at[h, 0], ax2(1))
-        far_m = send(two(Gs, 0, 1), Q2.at[h, 1], ax2(3))
+        far_p = send(two(Gs, 0, 0), Q2.at[h, 0], ax2(1), ks)
+        far_m = send(two(Gs, 0, 1), Q2.at[h, 1], ax2(3), ks)
         total(1)
-        near_p = send(two(Gs, 1, 1), Q1.at[h, 0, 1], ax2(1))
+        near_p = send(two(Gs, 1, 1), Q1.at[h, 0, 1], ax2(1), ks)
         yield
         far_p.wait_recv()
         two(Gs, 1, 0)[...] = (two(G, 1, 0)[...] + Q2[h, 0].astype(F32)).astype(BF16)
-        both_p = send(two(Gs, 1, 0), Q1.at[h, 0, 0], ax2(1))
+        both_p = send(two(Gs, 1, 0), Q1.at[h, 0, 0], ax2(1), ks)
         yield
         arrived(1)
         total(2)
-        near_m = send(two(Gs, 2, 0), Q1.at[h, 1, 0], ax2(3))
+        near_m = send(two(Gs, 2, 0), Q1.at[h, 1, 0], ax2(3), ks)
         far_m.wait_recv()
         two(Gs, 2, 1)[...] = (two(G, 2, 1)[...] + Q2[h, 1].astype(F32)).astype(BF16)
-        both_m = send(two(Gs, 2, 1), Q1.at[h, 1, 1], ax2(3))
+        both_m = send(two(Gs, 2, 1), Q1.at[h, 1, 1], ax2(3), ks)
         total(3)
         yield
         for cp in (near_p, near_m, both_p, both_m):
@@ -316,7 +325,7 @@
         two(Gs, 3, away)[...] = (
             two(G, 3, away)[...] + Q1[h, 0, away].astype(F32) + Q1[h, 1, away].astype(F32)
         ).astype(BF16)
-        last = send(two(Gs, 3, away), Z3.at[h], at_z(4))
+        last = send(two(Gs, 3, away), Z3.at[h], at_z(4), ks)
         yield
         mine = two(G, 3, zh)[...] + Q1[h, 0, zh].astype(F32) + Q1[h, 1, zh].astype(F32)
         last.wait_recv()
@@ -393,13 +402,14 @@
             for j in range(8):
                 AT[j % 2, j // 2, pl.ds(32 * b, 32)] = t[32 * j : 32 * (j + 1)]
 
-    def error_term():
-        eb = jnp.concatenate([nt(basis[...], err[...], HI)] * 4, axis=1)
+    def error_term(b3):
+        eb = fold3(nt(b3, split3(err[...])))
+        eb = jnp.concatenate([eb[:, :32] + (eb[:, 32:64] + eb[:, 64:])] * 4, axis=1)
         col = lax.broadcasted_iota(jnp.int32, (R, D), 1)
         return jnp.where(col // 32 == i, jnp.concatenate([eb] * 16, axis=1), 0.0)
 
-    def left_factor(eb):
-        u = fold3(nt(split3(basis[...]), go[...]))
+    def left_factor(b3, eb):
+        u = fold3(nt(b3, go[...]))
         al.wait()
         p = fold3(nn(split3(u), acts[...]))
         put(0, (p * scale + eb) * (1.0 / GROUPS))
@@ -469,15 +479,16 @@
 
     wl[0].wait()
     bl.wait()
+    b3 = split3(basis[...])
     el.wait()
-    eb = error_term()
+    eb = error_term(b3)
     pl.when(source)(wl[1].wait)
     pl.semaphore_wait(barrier, len(peers))
     adv(*own_w)
     wz = send(WA.at[zh, y, x, c], WA.at[zh, y, x, c], mirror)
     adv(z_w)
     gl.wait()
-    left_factor(eb)
+    left_factor(b3, eb)
     adv(red[0])
     got = [send(go, go_tw, twin)]
     transpose_acts()
@@ -487,19 +498,19 @@
     adv(z_w)
     grad_own(2)
     grad_own(1)
+    adv(red[0])
     wz.wait_recv()
     adv(*oth_w)
     grad_own(3)
+    adv(*own_w)
+    adv(z_w)
     grad_own(0)
-    adv(red[0])
-    adv(*own_w)
-    adv(z_w)
     adv(*oth_w)
     for cp in got:
         cp.wait_recv()
     grad_twin(2)
+    adv(red[0])
     adv(*own_w)
-    adv(red[0])
     adv(grads[0])
     adv(grads[0])
     grad_twin(1)
@@ -509,23 +520,22 @@
     adv(grads[1])
     adv(grads[1])
     adv(grads[1])
-    adv(z_w)
     adv(red[0])
+    adv(z_w)
     adv(red[0])
     right_factor()
     adv(red[1])
-    adv(grads[0])
     gram()
     adv(red[1])
-    adv(grads[1])
+    adv(*grads)
     adv(*grads)
     factor(0, 16)
     adv(z_w)
     adv(*grads)
-    adv(*oth_w)
     factor(16, 32)
     adv(red[1])
     adv(*grads)
+    adv(*oth_w)
     adv(*own_w)
     factor(32, 48)
     adv(*own_w)
@@ -534,14 +544,13 @@
     adv(red[1])
     ortho = nn(M[:, R:], my_rows(0), HI).T
     adv(*grads)
-    adv(z_w)
-    adv(*grads)
-    adv(z_w)
-    grad_acts(zh, 0)
+    adv(*grads)
+    adv(z_w)
+    adv(z_w)
+    grad_acts(zh, 0, 1)
     adv(red[1])
-    adv(*grads)
     adv(*oth_w)
-    grad_acts(zh, 1)
+    adv(*grads)
     adv(red[1])
     qf = nn(M[:, R:], full(1), HI)
     qt[...] = qf
@@ -554,7 +563,7 @@
     adv(*grads)
     res[...] = res[...] + err[...] - ap
     drain()
-    assert count[0] <= SEMS, count[0]
+    assert count[0] == RECV and count[1] == SEND, count
     for g in own_w + oth_w + [z_w] + grads + red:
         assert next(g, 0) == 0
 
@@ -602,8 +611,8 @@
             vm((2, 8, 4, 8, 512), F32),
             vm((R, 2 * R), F32),
             pltpu.SemaphoreType.DMA((6,)),
-            pltpu.SemaphoreType.DMA((SEMS,)),
-            pltpu.SemaphoreType.DMA((SEMS,)),
+            pltpu.SemaphoreType.DMA((SEND,)),
+            pltpu.SemaphoreType.DMA((RECV,)),
         ],
         compiler_params=pltpu.CompilerParams(
             collective_id=0, has_side_effects=True, vmem_limit_bytes=60 * 2**20

time: 73.1 us -> 70.2 us (0.960)
  Pallas kernels: 72.2 us -> 69.3 us
    pallas_call x1, Pallas kernels: 70.5 us -> 67.6 us  [shards(): pl.pallas_call(functools.partial(kernel, scale), out_shape=(vm((TOK, D),...]
where the time goes in v4:
time: 70.2 us; the launch traced here: 70.1 us
  Pallas kernels  69.3 us (99%)
  between operations  0.8 us (1%)
    pallas_call x1, Pallas kernels, shards(): pl.pallas_call(functools.partial(kernel, scale), out_shape=(vm((TOK, D),...  67.6 us
    pallas_call x1, Pallas kernels, shards(): pl.pallas_call(write_out, out_shape=(jax.ShapeDtypeStruct((TOK, D), BF16)...  1.69 us

profile of v4, /device:TPU:1, one launch (start us, length us, event | category | flops | bytes accessed | tf_op | source)
XLA Modules:
  0.0 70.1 jit_solution(15286738773472752942)
XLA Ops:
  0.6 67.6 %powersgd.1 = (bf16[512,2048]{1,0:T(8,128)(2,1)S(1)}, f32[32,2048]{1,0:T(8,128)S(1)}, f32[32,2048]{1,0:T(8,128)S(1)}, f32[64,2048]{1,0:T(8,128)S(1)}) custom-call(bf16[512,2048]{1,0:T(8,128)(2,1)} %acts_hbm.1, bf16[512,2048]{1,0:T(8,128)(2,1)} %go_hbm.1, bf16[32,2048]{1,0:T(8,128)(2,1)} %weight_hbm.1, f32[32,2048]{1,0:T(8,128)} %bitcast.5, f32[64,2048]{1,0:T(8,128)} %bitcast.4), custom_call_target="tpu_custom_call" | custom-call | tf_op jit(solution)/shard_map/powersgd/pallas_call | solution.py:583
  68.3 1.7 %write_out.1 = (bf16[512,2048]{1,0:T(8,128)(2,1)}, f32[32,2048]{1,0:T(8,128)}, f32[32,2048]{1,0:T(8,128)}, f32[64,2048]{1,0:T(8,128)}) custom-call(bf16[512,2048]{1,0:T(8,128)(2,1)S(1)} %get-tuple-element.12.a, f32[32,2048]{1,0:T(8,128)S(1)} %get-tuple-element.13.b, f32[32,2048]{1,0:T(8,128)S(1)} %get-tuple-element.14.c, f32[64,2048]{1,0:T(8,128)S(1)} %get-tuple-element.15.d), custom_call_target="tpu_custom_call" | custom-call | tf_op jit(solution)/shard_map/write_out/pallas_call | solution.py:622

commit v5 on v4

--- a/solution.py
+++ b/solution.py
@@ -540,16 +540,16 @@
     factor(32, 48)
     adv(*own_w)
     adv(z_w)
+    adv(red[1])
     factor(48, 64)
+    ortho = nn(M[:, R:], my_rows(0), HI).T
+    adv(*grads)
+    adv(*grads)
+    adv(z_w)
+    adv(z_w)
+    grad_acts(zh, 0, 1, 2, 3)
+    adv(*oth_w)
     adv(red[1])
-    ortho = nn(M[:, R:], my_rows(0), HI).T
-    adv(*grads)
-    adv(*grads)
-    adv(z_w)
-    adv(z_w)
-    grad_acts(zh, 0, 1)
-    adv(red[1])
-    adv(*oth_w)
     adv(*grads)
     adv(red[1])
     qf = nn(M[:, R:], full(1), HI)
@@ -557,7 +557,6 @@
     ap = nn(ortho, qf, HI)
     apv[...] = ap
     adv(*oth_w)
-    grad_acts(zh, 2, 3)
     adv(*oth_w)
     grad_acts(1 - zh, 0, 1, 2, 3)
     adv(*grads)

time: 70.2 us -> 69.8 us (level)
  no operation moved by 1% of the time
where the time goes in v5:
time: 69.8 us; the launch traced here: 69.7 us
  Pallas kernels  68.9 us (99%)
  between operations  0.8 us (1%)
    pallas_call x1, Pallas kernels, shards(): pl.pallas_call(functools.partial(kernel, scale), out_shape=(vm((TOK, D),...  67.2 us
    pallas_call x1, Pallas kernels, shards(): pl.pallas_call(write_out, out_shape=(jax.ShapeDtypeStruct((TOK, D), BF16)...  1.69 us

profile of v5, /device:TPU:1, one launch (start us, length us, event | category | flops | bytes accessed | tf_op | source)
XLA Modules:
  0.0 69.7 jit_solution(16690519089494868349)
XLA Ops:
  0.6 67.2 %powersgd.1 = (bf16[512,2048]{1,0:T(8,128)(2,1)S(1)}, f32[32,2048]{1,0:T(8,128)S(1)}, f32[32,2048]{1,0:T(8,128)S(1)}, f32[64,2048]{1,0:T(8,128)S(1)}) custom-call(bf16[512,2048]{1,0:T(8,128)(2,1)} %acts_hbm.1, bf16[512,2048]{1,0:T(8,128)(2,1)} %go_hbm.1, bf16[32,2048]{1,0:T(8,128)(2,1)} %weight_hbm.1, f32[32,2048]{1,0:T(8,128)} %bitcast.5, f32[64,2048]{1,0:T(8,128)} %bitcast.4), custom_call_target="tpu_custom_call" | custom-call | tf_op jit(solution)/shard_map/powersgd/pallas_call | solution.py:582
  67.8 1.7 %write_out.1 = (bf16[512,2048]{1,0:T(8,128)(2,1)}, f32[32,2048]{1,0:T(8,128)}, f32[32,2048]{1,0:T(8,128)}, f32[64,2048]{1,0:T(8,128)}) custom-call(bf16[512,2048]{1,0:T(8,128)(2,1)S(1)} %get-tuple-element.12.a, f32[32,2048]{1,0:T(8,128)S(1)} %get-tuple-element.13.b, f32[32,2048]{1,0:T(8,128)S(1)} %get-tuple-element.14.c, f32[64,2048]{1,0:T(8,128)S(1)} %get-tuple-element.15.d), custom_call_target="tpu_custom_call" | custom-call | tf_op jit(solution)/shard_map/write_out/pallas_call | solution.py:621
